TPU v7x, 128 devices: a whole 4x4x4 slice. The times are simulated.
128 devices in a mesh: var: 8 (over x_hi, z), seq: 16 (over x_lo, y, core).
Axes of the slice: x: 4 (x_hi: 2, x_lo: 2; x = x_hi * 2 + x_lo), y: 4, z: 4, core: 2. Of those that a mesh axis runs over, the one named last changes fastest.
Arguments:
- fields: bfloat16 [48, 4096, 1024], P('var', 'seq'), may hold values from -10 to 10
- var_bias: bfloat16 [48, 1024], P('var'), may hold values from -3 to 3
- agg_score: bfloat16 [1024, 16], replicated
- agg_value: bfloat16 [1024, 1024], P('seq'), may hold values from -0.1875 to 0.1875
- agg_out: bfloat16 [1024, 4096], P(None, 'var'), may hold values from -0.1875 to 0.1875
- norm_gain: float32 [4096], replicated, may hold values from 0.5 to 1.5
- w_query: bfloat16 [4096, 4096], P(None, 'var')
- w_key: bfloat16 [4096, 4096], P(None, 'var')
- w_value: bfloat16 [4096, 4096], P(None, 'var'), may hold values from -0.09375 to 0.09375
- w_out: bfloat16 [4096, 4096], P('var'), may hold values from -0.09375 to 0.09375
- w_back: bfloat16 [4096, 1024], P('var'), may hold values from -0.09375 to 0.09375
- var_gate: bfloat16 [48, 1024], P('var'), may hold values from 0.5 to 1.5
Outputs:
- mixed: bfloat16 [4096, 4096], P('seq', 'var')
- out_fields: bfloat16 [48, 4096, 1024], P('var', 'seq')
All inputs are finite; a program needn't handle non-finite values.
Results may differ from a plain program's by a relative error of at most 0.029.
Values may be sent and summed in bfloat16 or wider, within the bound.
A program may use at most 128 MiB of HBM per device.

v0:
```python
import math

import jax
import jax.numpy as jnp
from jax import lax
from jax.sharding import PartitionSpec as P

D = 4096
H = 32
HA = 16


def joined(value, axis, join):
    pieces = jax.tree.map(lambda part: lax.all_gather(part, axis), value)
    head = jax.tree.map(lambda part: part[0], pieces)
    tail = jax.tree.map(lambda part: part[1:], pieces)
    running, _ = lax.scan(lambda running, share: (join(running, share), None), head, tail)
    return running


def combine_partials(first, second):
    peak = jnp.maximum(first[0], second[0])
    scale_one = jnp.exp(first[0] - peak)
    scale_two = jnp.exp(second[0] - peak)
    reach = first[2].shape[1] // peak.shape[1]
    total = first[1] * scale_one + second[1] * scale_two
    summed = first[2] * jnp.repeat(scale_one, reach, axis=1) + second[2] * jnp.repeat(
        scale_two, reach, axis=1
    )
    return (peak, total, summed)


def per_device(
    fields,
    var_bias,
    agg_score,
    agg_value,
    agg_out,
    norm_gain,
    w_query,
    w_key,
    w_value,
    w_out,
    w_back,
    var_gate,
):
    var_count, tok_count, width = fields.shape
    agg_dim = width // HA
    head_dim = D // H
    local_width = w_query.shape[1]
    local_heads = local_width // head_dim
    scale = 1.0 / math.sqrt(head_dim)
    value_full = lax.all_gather(agg_value, "seq", axis=0, tiled=True)
    embedded = (fields.astype(jnp.float32) + var_bias.astype(jnp.float32)[:, None, :]).astype(
        jnp.bfloat16
    )
    score = jnp.einsum("vte,eh->vth", embedded, agg_score, preferred_element_type=jnp.float32)
    values = jnp.dot(
        embedded.reshape(-1, width), value_full, preferred_element_type=jnp.float32
    ).astype(jnp.bfloat16)
    values = values.reshape(var_count, tok_count, HA, agg_dim)
    local_peak = jnp.max(score, axis=0)
    prob = jnp.exp(score - local_peak[None])
    total = jnp.sum(prob, axis=0)
    summed = jnp.einsum("vth,vthd->thd", prob, values.astype(jnp.float32)).reshape(tok_count, width)
    total, summed = (total, summed)
    peak, total, summed = joined((local_peak, total, summed), "var", combine_partials)
    agg = (summed / jnp.repeat(total, agg_dim, axis=1)).astype(jnp.bfloat16)
    own_hidden = jnp.dot(agg, agg_out, preferred_element_type=jnp.float32).astype(jnp.bfloat16)
    hidden = lax.all_gather(own_hidden, "var", axis=1, tiled=True)
    wide = hidden.astype(jnp.float32)
    mean = jnp.mean(wide, axis=1, keepdims=True)
    spread = jnp.mean((wide - mean) ** 2, axis=1, keepdims=True)
    normed = ((wide - mean) * lax.rsqrt(spread + 1e-05) * norm_gain[None, :]).astype(jnp.bfloat16)
    query = jnp.dot(normed, w_query, preferred_element_type=jnp.float32).astype(jnp.bfloat16)
    keys = jnp.dot(normed, w_key, preferred_element_type=jnp.float32).astype(jnp.bfloat16)
    vals = jnp.dot(normed, w_value, preferred_element_type=jnp.float32).astype(jnp.bfloat16)
    query = query.reshape(tok_count, local_heads, head_dim)
    all_keys, all_vals = (
        lax.all_gather(keys, "seq", axis=0, tiled=True),
        lax.all_gather(vals, "seq", axis=0, tiled=True),
    )
    all_keys = all_keys.reshape(-1, local_heads, head_dim)
    all_vals = all_vals.reshape(-1, local_heads, head_dim)
    scores = jnp.einsum("thd,shd->hts", query, all_keys, preferred_element_type=jnp.float32) * scale
    expo = jnp.exp(scores - jnp.max(scores, axis=2, keepdims=True))
    total_attn = jnp.sum(expo, axis=2)
    context = jnp.einsum(
        "hts,shd->thd", expo.astype(jnp.bfloat16), all_vals, preferred_element_type=jnp.float32
    )
    context = (
        (context / total_attn.T[:, :, None]).reshape(tok_count, local_width).astype(jnp.bfloat16)
    )
    partial_out = jnp.dot(context, w_out, preferred_element_type=jnp.float32)
    attended = lax.psum_scatter(partial_out, "var", scatter_dimension=1, tiled=True)
    mixed = (own_hidden.astype(jnp.float32) + attended).astype(jnp.bfloat16)
    back_part = jnp.dot(mixed, w_back, preferred_element_type=jnp.float32)
    back = lax.psum(back_part, "var")
    out_fields = (
        fields.astype(jnp.float32) + var_gate.astype(jnp.float32)[:, None, :] * back[None]
    ).astype(jnp.bfloat16)
    return (mixed, out_fields)


def solution(mesh):
    in_specs = (
        P("var", "seq", None),
        P("var", None),
        P(),
        P("seq", None),
        P(None, "var"),
        P(),
        P(None, "var"),
        P(None, "var"),
        P(None, "var"),
        P("var", None),
        P("var", None),
        P("var", None),
    )
    out_specs = (P("seq", "var"), P("var", "seq", None))
    return jax.shard_map(
        per_device, mesh=mesh, in_specs=in_specs, out_specs=out_specs, check_vma=False
    )
```

profile of v0, /device:TPU:0, one launch (start us, length us, event | category | flops | bytes accessed | tf_op | source)
XLA Modules:
  0.0 565.8 jit_solution(7693001359509680680)
XLA Ops:
  8.7 2.8 fusion.10
  11.5 1.7 copy-done.1
  14.2 32.1 %all-gather.8.cloned.1.call-done = bf16[1024,1024]{1,0:T(8,128)(2,1)} async-done(((bf16[64,1024]{1,0:T(8,128)(2,1)}), bf16[1024,1024]{1,0:T(8,128)(2,1)}) %all-gather.8.cloned.1.call-update) | async-done | bytes 2097168 | tf_op jit(solution)/shard_map/all_gather | solution.py:53
  46.3 7.6 %convolution_convert_fusion = bf16[1536,1024]{1,0:T(8,128)(2,1)} fusion(bf16[1536,1024]{1,0:T(8,128)(2,1)} %bitcast.93, bf16[1024,1024]{1,0:T(8,128)(2,1)} %all-gather.8.cloned.1.call-done), kind=kOutput, calls=%fused_computation.35 | convolution fusion | flops 3222798336 | bytes 8388608 | tf_op jit(solution)/shard_map/dot_general | solution.py:58
  53.9 4.6 copy.26
  58.5 7.5 %reshape.50 = bf16[6,256,16,64]{1,0,3,2:T(8,128)(2,1)} reshape(bf16[1536,1024]{0,1:T(8,128)(2,1)} %copy.26) | data formatting | bytes 6291456 | tf_op jit(solution)/shard_map/reshape | solution.py:61
  66.0 5.0 multiply_reduce_fusion.1
  71.0 1.3 copy.27
  72.4 34.8 %all-gather.1 = f32[2048,16]{0,1:T(8,128)S(1)} all-gather(f32[256,16]{0,1:T(8,128)S(1)} %get-tuple-element.77), channel_id=3, replica_groups=mesh['var'=8,'seq'=16] {'var'}, dimensions={0}, use_global_device_ids=true | all-gather | bytes 147456 | tf_op jit(solution)/shard_map/all_gather | solution.py:14
  107.2 34.9 %all-gather = f32[2048,16]{0,1:T(8,128)S(1)} all-gather(f32[256,16]{0,1:T(8,128)S(1)} %get-tuple-element.78), channel_id=2, replica_groups=mesh['var'=8,'seq'=16] {'var'}, dimensions={0}, use_global_device_ids=true | all-gather | bytes 147456 | tf_op jit(solution)/shard_map/all_gather | solution.py:14
  142.2 38.8 %all-gather.10.cloned.1.call-done = f32[8,256,1024]{2,1,0:T(8,128)} async-done(((f32[1,256,1024]{2,1,0:T(8,128)}), f32[8,256,1024]{2,1,0:T(8,128)}) %all-gather.10.cloned.1.call-update) | async-done | bytes 8388624 | tf_op jit(solution)/shard_map/all_gather | solution.py:14
  181.1 1.3 slice_bitcast_fusion
  182.4 1.3 copy.28
  183.7 7.5 %slice.33 = f32[7,256,1024]{2,1,0:T(8,128)} slice(f32[8,256,1024]{2,1,0:T(8,128)} %all-gather.10.cloned.1.call-done), slice={[1:8], [0:256], [0:1024]} | slice | bytes 14680064 | tf_op jit(solution)/shard_map/slice | solution.py:16
  191.2 28.4 %while.14 = (s32[]{:T(128)}, f32[256,16]{0,1:T(8,128)S(1)}, f32[256,16]{0,1:T(8,128)S(1)}, f32[256,1024]{0,1:T(8,128)}, f32[7,256,16]{1,0,2:T(8,128)S(1)}, /*ind...) while((s32[]{:T(128)}, f32[256,16]{0,1:T(8,128)S(1)}, f32[256,16]{0,1:T(8,128)S(1)}, ...), condition=%wide.region_3.4_spmd, body=%wide.region_2.3_spmd.sunk | while | flops 811010 | bytes 7569501 | solution.py:17
  191.2 1.3 constant_dynamic-slice_fusion.6
  192.9 2.3 fusion.62
  195.3 1.3 constant_dynamic-slice_fusion.6
  196.9 2.3 fusion.62
  199.3 1.3 constant_dynamic-slice_fusion.6
  201.0 2.3 fusion.62
  203.4 1.3 constant_dynamic-slice_fusion.6
  205.0 2.3 fusion.62
  207.4 1.3 constant_dynamic-slice_fusion.6
  209.1 2.3 fusion.62
  211.5 1.3 constant_dynamic-slice_fusion.6
  213.1 2.3 fusion.62
  215.5 1.3 constant_dynamic-slice_fusion.6
  217.2 2.3 fusion.62
  219.5 1.3 fusion.24
  220.8 2.4 convolution_convert_fusion.4
  223.3 52.4 %all-gather.12.cloned.1.call-done = bf16[256,4096]{1,0:T(8,128)(2,1)} async-done(((bf16[256,512]{1,0:T(8,128)(2,1)}), bf16[256,4096]{1,0:T(8,128)(2,1)}) %all-gather.12.cloned.1.call-update) | async-done | bytes 2097168 | tf_op jit(solution)/shard_map/all_gather | solution.py:70
  275.7 2.1 convert_reduce_fusion
  277.8 2.3 fusion.14
  280.1 4.2 convolution_convert_fusion.1
  284.4 4.2 convolution_convert_fusion.3
  288.6 3.5 fusion.23
  292.1 27.5 %all-gather.16.cloned.1.call-done = bf16[4096,512]{1,0:T(8,128)(2,1)} async-done(((bf16[256,512]{1,0:T(8,128)(2,1)}), bf16[4096,512]{1,0:T(8,128)(2,1)}) %all-gather.16.cloned.1.call-update) | async-done | bytes 4194320 | tf_op jit(solution)/shard_map/all_gather | solution.py:80
  319.6 10.3 %multiply_reduce_fusion = (f32[4,256]{1,0:T(4,128)S(1)}, f32[4,256,4096]{2,1,0:T(8,128)}) fusion(bf16[32,4,8,128]{3,2,1,0:T(8,128)(2,1)S(1)} %fusion.23, bf16[4096,512]{1,0:T(8,128)(2,1)} %all-gather.16.cloned.1.call-done), kind=kOutput, calls=%fused_computation.14 | convolution fusion | flops 1082129408 | bytes 21237760 | tf_op jit(solution)/shard_map/thd,shd->hts/dot_general | solution.py:85
  329.9 8.8 %fusion.4 = f32[4,256]{1,0:T(4,128)S(1)} fusion(f32[4,256,4096]{2,1,0:T(8,128)} %get-tuple-element.81, f32[4,256]{1,0:T(4,128)S(1)} %get-tuple-element.80), kind=kLoop, calls=%fused_computation.15 | loop fusion | flops 12581888 | bytes 16785408 | tf_op jit(solution)/shard_map/reduce_sum | solution.py:87
  338.7 20.4 %all-gather.14.cloned.1.call-done = bf16[4096,512]{1,0:T(8,128)(2,1)} async-done(((bf16[256,512]{1,0:T(8,128)(2,1)}), bf16[4096,512]{1,0:T(8,128)(2,1)}) %all-gather.14.cloned.1.call-update) | async-done | bytes 4194320 | tf_op jit(solution)/shard_map/all_gather | solution.py:81
  359.2 6.4 %copy.41 = bf16[4096,512]{0,1:T(8,128)(2,1)} copy(bf16[4096,512]{1,0:T(8,128)(2,1)} %all-gather.14.cloned.1.call-done) | data formatting | bytes 8388608 | tf_op jit(solution)/shard_map/reshape | solution.py:84
  365.5 10.6 %fusion.28 = bf16[256,4,128]{0,2,1:T(8,128)(2,1)S(1)} fusion(bf16[4096,4,128]{0,2,1:T(8,128)(2,1)} %bitcast.94, f32[4,256,4096]{2,1,0:T(8,128)} %get-tuple-element.81, f32[4,256]{1,0:T(4,128)S(1)} %get-tuple-element.80, f32[256,4]{0,1:T(4,128)S(1)} %bitcast.97), kind=kOutput, calls=%fused_computation.46 | convolution fusion | flops 1086586880 | bytes 21241856 | tf_op jit(solution)/shard_map/hts,shd->thd/dot_general | solution.py:88
  376.1 3.2 fusion.43
  379.4 84.8 %reduce-scatter.2.cloned.1.call-done = f32[256,512]{1,0:T(8,128)} async-done(((f32[256,4096]{1,0:T(8,128)}), f32[256,512]{1,0:T(8,128)}) %reduce-scatter.2.cloned.1.call-update) | async-done | bytes 524304 | tf_op jit(solution)/shard_map/reduce_scatter | solution.py:95
  465.4 1.4 fusion.44
  466.9 87.3 %all-reduce.2.cloned.1.call-done = f32[256,1024]{1,0:T(8,128)} async-done(((f32[256,1024]{1,0:T(8,128)}), f32[256,1024]{1,0:T(8,128)}) %all-reduce.2.cloned.1.call-update) | async-done | bytes 1048592 | tf_op jit(solution)/shard_map/psum | solution.py:98
  554.1 4.8 fusion.11
  (66 shorter events, 6.8 us)
Async XLA Ops:
  7.2 458.2 %copy-start = (bf16[512,1024]{1,0:T(8,128)(2,1)S(1)}, bf16[512,1024]{1,0:T(8,128)(2,1)}, u32[]{:S(2)}) copy-start(bf16[512,1024]{1,0:T(8,128)(2,1)} %param.24) | copy-start | bytes 3145732
  7.2 5.9 %copy-start.6 = (bf16[1024,16]{0,1:T(8,128)(2,1)S(1)}, bf16[1024,16]{0,1:T(8,128)(2,1)}, u32[]{:S(2)}) copy-start(bf16[1024,16]{0,1:T(8,128)(2,1)} %param.16) | copy-start | bytes 98308
  7.2 39.1 %all-gather.8.cloned.1.call-start = ((), (), s32[]{:S(2)}) async-start(), calls=%async_computation.1 | async-start | bytes 2228224 | tf_op jit(solution)/shard_map/all_gather | solution.py:53
  7.9 173.2 %all-gather.10.cloned.1.call-start = ((), (), s32[]{:S(2)}) async-start(), calls=%async_computation.2 | async-start | bytes 9437184 | tf_op jit(solution)/shard_map/all_gather | solution.py:14
  11.5 1.7 copy-start.1
  72.4 203.3 %all-gather.12.cloned.1.call-start = ((), (), s32[]{:S(2)}) async-start(), calls=%async_computation.3 | async-start | bytes 2359296 | tf_op jit(solution)/shard_map/all_gather | solution.py:70
  219.5 60.6 %copy-start.8 = (f32[4096]{0:T(1024)S(1)}, f32[4096]{0:T(1024)}, u32[]{:S(2)}) copy-start(f32[4096]{0:T(1024)} %param.19) | copy-start | bytes 49156
  223.2 96.4 %all-gather.16.cloned.1.call-start = ((), (), s32[]{:S(2)}) async-start(), calls=%async_computation.5 | async-start | bytes 4456448 | tf_op jit(solution)/shard_map/all_gather | solution.py:80
  275.7 4.4 copy-start.3
  284.3 74.8 %all-gather.14.cloned.1.call-start = ((), (), s32[]{:S(2)}) async-start(), calls=%async_computation.4 | async-start | bytes 4456448 | tf_op jit(solution)/shard_map/all_gather | solution.py:81
  288.6 175.7 %reduce-scatter.2.cloned.1.call-start = ((), (), s32[]{:S(2)}) async-start(), calls=%async_computation.6 | async-start | bytes 4718592 | tf_op jit(solution)/shard_map/reduce_scatter | solution.py:95
  365.5 10.6 %copy-start.2 = (bf16[512,4096]{1,0:T(8,128)(2,1)S(1)}, bf16[512,4096]{1,0:T(8,128)(2,1)}, u32[]{:S(2)}) copy-start(bf16[512,4096]{1,0:T(8,128)(2,1)} %param.23) | copy-start | bytes 12582916
  379.4 84.9 %copy-start.5 = (bf16[256,512]{1,0:T(8,128)(2,1)S(1)}, bf16[256,512]{1,0:T(8,128)(2,1)}, u32[]{:S(2)}) copy-start(bf16[256,512]{1,0:T(8,128)(2,1)} %convolution_convert_fusion.4) | copy-start | bytes 786436
  379.4 87.5 %copy-start.7 = (bf16[6,1024]{1,0:T(8,128)(2,1)S(1)}, bf16[6,1024]{1,0:T(8,128)(2,1)}, u32[]{:S(2)}) copy-start(bf16[6,1024]{1,0:T(8,128)(2,1)} %param.25) | copy-start | bytes 36868
  379.4 174.7 %all-reduce.2.cloned.1.call-start = ((), (), s32[]{:S(2)}) async-start(), calls=%async_computation.7 | async-start | bytes 2097152 | tf_op jit(solution)/shard_map/psum | solution.py:98
  465.4 93.5 %copy-start.4 = (bf16[256,512]{1,0:T(8,128)(2,1)}, bf16[256,512]{1,0:T(8,128)(2,1)S(1)}, u32[]{:S(2)}) copy-start(bf16[256,512]{1,0:T(8,128)(2,1)S(1)} %add_convert_fusion) | copy-start | bytes 786436
Sparse Core Ops, SparseCore 0:
  9.7 36.4 all-gather.7
  72.5 108.5 all-gather.9
  223.4 52.2 all-gather.11
  284.4 35.1 all-gather.15
  321.7 37.3 all-gather.13
  379.5 84.6 reduce-scatter.1
  467.5 86.5 all-reduce.1
where the time goes:
time: 567 us; the launch traced here: 566 us
  waiting for transfers between devices  344 us (61%)
  blocking collectives  69.7 us (12%)
  matrix products  48.3 us (9%)
  other arithmetic  45.6 us (8%)
  local copies, waits for them, and re-layouts  43.4 us (8%)
  between operations  14.3 us (3%)
    psum x1, waiting for transfers between devices, per_device(): back = lax.psum(back_part, 'var')  87.3 us
    reduce_scatter x1, waiting for transfers between devices, per_device(): lax.psum_scatter(partial_out, 'var', scatter_dimension=1, tiled=True)  84.8 us
    all_gather x2, blocking collectives, joined(): pieces = jax.tree.map(lambda part: lax.all_gather(part, axis), value)  69.7 us
    all_gather x1, waiting for transfers between devices, per_device(): hidden = lax.all_gather(own_hidden, 'var', axis=1, tiled=True)  52.4 us
    all_gather x1, waiting for transfers between devices, joined(): pieces = jax.tree.map(lambda part: lax.all_gather(part, axis), value)  38.8 us
    all_gather x1, waiting for transfers between devices, per_device(): value_full = lax.all_gather(agg_value, 'seq', axis=0, tiled=True)  32.1 us
    all_gather x1, waiting for transfers between devices, per_device(): lax.all_gather(keys, 'seq', axis=0, tiled=True)  27.5 us
    all_gather x1, waiting for transfers between devices, per_device(): lax.all_gather(vals, 'seq', axis=0, tiled=True)  20.4 us
  transfers between devices with their start and end apart: 7, of which 7 were waited for; matrix products, arithmetic and copies ran while one was open for 6% of the time, Pallas kernels for 0%

commit v1 on v0

v1 whole, which is shorter than its diff:
```python
import functools
import math

import jax
import jax.numpy as jnp
from jax import lax
from jax.experimental import pallas as pl
from jax.experimental.pallas import tpu as pltpu
from jax.sharding import PartitionSpec as P

D = 4096
H = 32
HA = 16
E = 1024
NV = 8
NS = 16
LV = 6
T = 256
W = 512
HD = 128
F32 = jnp.float32
BF = jnp.bfloat16
MESH = pl.DeviceIdType.MESH

VAR_OFF = [(1, 2), (1, 1), (1, 3), (0, 2), (1, 0), (0, 1), (0, 3)]
Z_OFF = [(0, 2), (0, 1), (0, 3)]
Z_NEXT = [(0, 1), (0, 3)]
D_OFF = [(1, 2)] + Z_OFF
SEQ_OFF = [(1, 2), (1, 1), (1, 3), (0, 2), (1, 0), (0, 1), (0, 3)]

A, AF, ST, WX, OX = range(5)
PIECES = 4
WZ = 5
WS = WZ + PIECES
B, C, DG, K, KF, V, VF, Q, CX, XC, F, G, GG = range(WS + PIECES, WS + PIECES + 26, 2)
ROWS = WS + PIECES + 26
TH = T // 2


def rem(a, n):
    return lax.rem(a, jnp.int32(n))


def body(
    fields_h, bias_r, sw_r, av_h, ao_h, gain_r, wq_h, wk_h, wv_h, wo_h, wb_h,
    gate_r,
    mixed_r, back_r, gate_out,
    emb, av, ao, aox, wq, wk, wv, wo, wox, wb,
    e2, prob, stat, cat, bsend, brecv, agg, hid, macc, gsc, gws, off, st1, st2,
    ks, vs, qs, kb, vb, qb, sc, am, al, aa, cs, cb, cbx, fsend, frecv, fown, gsend, grecv, gb,
    ld, ssem, rsem,
):
    me_v = lax.axis_index("var")
    me_s = lax.axis_index("seq")
    xh, z = me_v // 4, rem(me_v, 4)
    xl, y, c = me_s // 8, rem(me_s // 2, 4), rem(me_s, 2)

    def var_of(o, sign=1):
        return rem(xh + o[0], 2) * 4 + rem(z + 4 + sign * o[1], 4)

    def seq_of(o, sign=1):
        return rem(xl + o[0], 2) * 8 + rem(y + 4 + sign * o[1], 4) * 2 + c

    sib = (me_v, xl * 8 + y * 2 + (1 - c))
    near = ((1 - xh) * 4 + z, (1 - xl) * 8 + y * 2 + c)
    part = ((1 - xh) * 4 + z, me_s)

    loads = {}

    def load(name, i, src, dst):
        cp = pltpu.make_async_copy(src, dst, ld.at[i])
        cp.start()
        loads[name] = cp

    av_own = av.at[pl.ds(pl.multiple_of(me_s * 64, 64), 64), :]
    load("av", 0, av_h, av_own)
    load("ao", 2, ao_h, ao)
    load("fields", 1, fields_h, emb)

    bar = pltpu.get_barrier_semaphore()
    for o in VAR_OFF:
        pl.semaphore_signal(bar, inc=1, device_id=(var_of(o), me_s), device_id_type=MESH)
    for o in SEQ_OFF:
        pl.semaphore_signal(bar, inc=1, device_id=(me_v, seq_of(o)), device_id_type=MESH)
    pl.semaphore_signal(bar, inc=1, device_id=sib, device_id_type=MESH)
    pl.semaphore_signal(bar, inc=1, device_id=near, device_id_type=MESH)
    for i in range(1, 4):
        pl.semaphore_signal(
            bar, inc=1, device_id=(part[0], seq_of((0, i))), device_id_type=MESH
        )
    pl.semaphore_wait(bar, 19)

    def remote(src, dst, ph, j, dev):
        return pltpu.make_async_remote_copy(
            src_ref=src, dst_ref=dst, send_sem=ssem.at[ph, j], recv_sem=rsem.at[ph, j],
            device_id=dev, device_id_type=MESH,
        )

    def seq_send(ph, src_of, dst):
        cps = []
        for j, o in enumerate(SEQ_OFF):
            cp = remote(src_of(o), dst(me_s), ph, j, (me_v, seq_of(o)))
            cp.start()
            cps.append(cp)
        return cps

    def seq_forward(ph, cps, dst):
        fw = []
        cp = remote(dst(me_s), dst(me_s), ph, 7, sib)
        cp.start()
        fw.append(cp)
        for j in reversed(range(7)):
            cps[j].wait_recv()
            s = seq_of(SEQ_OFF[j], -1)
            cp = remote(dst(s), dst(s), ph, j, sib)
            cp.start()
            fw.append(cp)
        return fw

    pending = []

    def var_scatter(ph, send, recv):
        cps = []
        for j, o in enumerate(VAR_OFF):
            pv = var_of(o)
            cp = remote(send.at[pv], recv.at[j], ph, j, (pv, me_s))
            cp.start()
            cps.append(cp)
        pending.extend(cps)
        return cps

    def var_gather(ph, buf, offs=VAR_OFF):
        cps = []
        for j, o in enumerate(offs):
            cp = remote(buf.at[me_v], buf.at[me_v], ph, j, (var_of(o), me_s))
            cp.start()
            cps.append(cp)
        pending.extend(cps)
        return cps

    gate_out[...] = gate_r[...].astype(F32)
    for p in range(NV):
        gsc[p] = jnp.broadcast_to(gain_r[p * W : (p + 1) * W].reshape(1, W), (8, W))

    loads["av"].wait()
    av_slot = lambda s: av.at[pl.ds(pl.multiple_of(s * 64, 64), 64), :]
    a_cps = seq_send(A, lambda o: av_slot(me_s), av_slot)
    pending.extend(a_cps)
    load("wk", 3, wk_h, wk)
    load("wv", 4, wv_h, wv)
    load("wq", 5, wq_h, wq)
    load("wo", 6, wo_h, wo)
    load("wb", 7, wb_h, wb)

    PR = E // 2 // PIECES

    def piece(i, core):
        return pl.ds(pl.multiple_of(core * (E // 2) + i * PR, PR), PR)

    loads["ao"].wait()
    wx = []
    for i in range(PIECES):
        cp = remote(ao.at[piece(i, c), :], aox.at[z, piece(i, c), :], WX, i, near)
        cp.start()
        wx.append(cp)
    pending.extend(wx)

    krow = lax.broadcasted_iota(jnp.int32, (128, E), 0)
    kcol = lax.broadcasted_iota(jnp.int32, (128, E), 1)
    e2[...] = jnp.where((rem(krow, 16) == kcol // 64) & (krow < 32), 1.0, 0.0).astype(BF)
    loads["fields"].wait()
    sw = sw_r[...]
    nt = (((1,), (1,)), ((), ()))
    for v in range(LV):
        b = bias_r[v : v + 1, :].astype(F32)

        def embed(r, _, v=v, b=b):
            rows = pl.ds(pl.multiple_of(r * 32, 32), 32)
            emb[v, rows, :] = (emb[v, rows, :].astype(F32) + b).astype(BF)
            return 0

        lax.fori_loop(0, T // 32, embed, 0)
        prob[v] = lax.dot_general(emb[v], sw, nt, preferred_element_type=F32)
    peak = prob[0]
    for v in range(1, LV):
        peak = jnp.maximum(peak, prob[v])
    total = jnp.zeros_like(peak)
    for v in range(LV):
        p = jnp.exp(prob[v] - peak)
        prob[v] = p
        total = total + p
    stat[me_v] = jnp.concatenate(
        [peak, total, jnp.zeros((T, 96), F32)], axis=1
    ).T[:32, :]
    s_cps = var_gather(ST, stat)
    wz = []
    ws = []

    def piece_on(i):
        wx[i].wait_recv()
        rows = piece(i, c)
        for j, o in enumerate(Z_NEXT):
            cp = remote(aox.at[z, rows, :], aox.at[z, rows, :], WZ + i, j, (var_of(o), me_s))
            cp.start()
            wz.append(cp)
            pending.append(cp)
        cp = remote(aox.at[z, rows, :], aox.at[z, rows, :], WS + i, 2, sib)
        cp.start()
        ws.append(cp)
        pending.append(cp)

    for i in range(PIECES):
        piece_on(i)
    a_fw = seq_forward(AF, a_cps, av_slot)
    pending.extend(a_fw)
    for cp in s_cps:
        cp.wait_recv()
    top = stat[0, :16, :]
    for i in range(1, NV):
        top = jnp.maximum(top, stat[i, :16, :])
    tot = jnp.zeros_like(top)
    for i in range(NV):
        tot = tot + stat[i, 16:, :] * jnp.exp(stat[i, :16, :] - top)
    scale = jnp.exp(stat[me_v, :16, :] - top) / tot
    fac = jnp.concatenate([scale, jnp.zeros((112, T), F32)], axis=0).T[:, :16]
    for v in range(LV):
        w = prob[v] * fac
        hi = w.astype(BF).astype(F32)
        cat[v] = jnp.concatenate([hi, w - hi, jnp.zeros((T, 96), F32)], axis=1).astype(BF)
    for cp in a_fw:
        cp.wait_recv()

    def values(hf):
        half = slice(hf * TH, (hf + 1) * TH)
        ev = emb[:, half, :].reshape(LV * TH, E)
        ct = cat[:, half, :].reshape(LV * TH, 128)

        def tile(n, _):
            cols = pl.ds(pl.multiple_of(n * 256, 256), 256)
            wide = jnp.dot(ct, e2[:, cols], preferred_element_type=F32)
            vals = jnp.dot(ev, av[:, cols], preferred_element_type=F32)
            s = jnp.sum((wide * vals).reshape(LV, TH, 256), axis=0).astype(BF)
            bsend[hf, 2 * n] = s[:, :128]
            bsend[hf, 2 * n + 1] = s[:, 128:]
            return 0

        lax.fori_loop(0, 4, tile, 0)

    b_cps = []
    for hf in range(2):
        values(hf)
        b_cps.append(var_scatter(B + hf, bsend.at[hf], brecv.at[hf]))

    loads["wo"].wait()
    mine_rows = pl.ds(pl.multiple_of(c * (W // 2), W // 2), W // 2)
    far_cols = pl.ds(pl.multiple_of((1 - xh) * (D // 2), D // 2), D // 2)
    ox = remote(wo.at[mine_rows, far_cols], wox.at[mine_rows, :], OX, 0, near)
    ox.start()
    pending.append(ox)

    for i in range(PIECES):
        rows = piece(i, c)
        for j, o in enumerate(Z_NEXT):
            wz[2 * i + j].wait_recv()
            zz = rem(z + 4 - o[1], 4)
            cp = remote(aox.at[zz, rows, :], aox.at[zz, rows, :], WS + i, j, sib)
            cp.start()
            ws.append(cp)
            pending.append(cp)

    for name in ("wk", "wv", "wq"):
        loads[name].wait()

    def gain_sums(p, _):
        g = gsc[p]
        hi = g.astype(BF).astype(F32)
        rows = pl.ds(pl.multiple_of(p * W, W), W)
        top = lax.broadcasted_iota(jnp.int32, (16, W), 0) < 8
        g2 = jnp.where(top, jnp.concatenate([hi, hi], axis=0), jnp.concatenate([g - hi, g - hi], axis=0))
        g2 = g2.astype(BF)
        for i, w in enumerate((wk, wv, wq)):
            o = jnp.dot(g2, w[rows, :], preferred_element_type=F32)
            gws[i] = gws[i] + o[0:1, :] + o[8:9, :]
        return 0

    gws[...] = jnp.zeros_like(gws)
    lax.fori_loop(0, NV, gain_sums, 0)

    c_cps = []
    for hf in range(2):
        tot = bsend[hf, me_v].astype(F32)
        for j in reversed(range(7)):
            b_cps[hf][j].wait_recv()
            tot = tot + brecv[hf, j].astype(F32)
        agg[hf, me_v] = tot.astype(BF)
        c_cps.append(var_gather(C + hf, agg.at[hf]))

    d_cps = []
    fulls = []
    for hf in range(2):
        for cp in c_cps[hf]:
            cp.wait_recv()
        full = jnp.concatenate([agg[hf, p] for p in range(NV)], axis=1)
        hid[hf, me_v] = jnp.dot(full, ao[...], preferred_element_type=F32).astype(BF)
        d_cps.append(var_gather(DG + hf, hid.at[hf], D_OFF))
    for cp in ws:
        cp.wait_recv()

    def other_side(i, _):
        zz = rem(z + 3 + i, 4)
        for hf in range(2):
            full = jnp.concatenate([agg[hf, p] for p in range(NV)], axis=1)
            hid[hf, (1 - xh) * 4 + zz] = jnp.dot(
                full, aox[zz], preferred_element_type=F32
            ).astype(BF)
        return 0

    lax.fori_loop(0, 3, other_side, 0)

    def shift(hf):
        t = jnp.zeros((TH, W), F32)
        for i in range(4):
            vv = me_v if i == 3 else (1 - xh) * 4 + rem(z + 3 + i, 4)
            t = t + hid[hf, vv].astype(F32)
        off[hf] = jnp.sum(t, axis=1, keepdims=True) * (1.0 / (4 * W))

    def take(hf, vv, first=False):
        d = hid[hf, vv].astype(F32) - off[hf]
        x = (d * gsc[vv, 0:1, :]).astype(BF)
        rows = pl.ds(pl.multiple_of(vv * W, W), W)
        for i, w in enumerate((wk, wv, wq)):
            o = jnp.dot(x, w[rows, :], preferred_element_type=F32)
            macc[hf, i] = o if first else macc[hf, i] + o
        s1 = d[:, 0:128]
        s2 = s1 * s1
        for n in range(1, 4):
            e = d[:, n * 128 : (n + 1) * 128]
            s1 = s1 + e
            s2 = s2 + e * e
        if not first:
            s1 = s1 + st1[hf]
            s2 = s2 + st2[hf]
        st1[hf] = s1
        st2[hf] = s2

    def statistics(hf):
        mean = jnp.sum(st1[hf], axis=1, keepdims=True) * (1.0 / D)
        sq = jnp.sum(st2[hf], axis=1, keepdims=True) * (1.0 / D)
        return mean, lax.rsqrt(jnp.maximum(sq - mean * mean, 0.0) + 1e-05)

    def project(i, out, hf, mean, inv):
        m = (macc[hf, i] - mean * gws[i]) * inv
        for h in range(4):
            out[hf, h] = m[:, h * HD : (h + 1) * HD].astype(BF)

    def slot(buf, hf):
        return lambda s: buf.at[hf, pl.ds(pl.multiple_of(s * TH, TH), TH), :]

    mine = pl.ds(pl.multiple_of(me_s * TH, TH), TH)

    def send_kv(ph, out, buf, hf):
        cps = seq_send(ph + hf, lambda o: out.at[hf, rem(y + o[1], 4)], slot(buf, hf))
        pending.extend(cps)
        buf[hf, mine, :] = out[hf, y]
        return cps

    def send_q(hf):
        cps = []
        for i in range(1, 4):
            h = rem(y + i, 4)
            cp = remote(
                qs.at[hf, h], qb.at[hf, pl.ds((4 - i) * TH, TH), :], Q + hf, i,
                (me_v, xl * 8 + h * 2 + c),
            )
            cp.start()
            cps.append(cp)
        pending.extend(cps)
        qb[hf, 0:TH, :] = qs[hf, y]
        return cps

    coef = math.log2(math.e) / math.sqrt(HD)
    KC = 512
    NK = NS * TH
    QT = 2 * TH

    def attend(hf, kh):
        def tile(i, _):
            base = 2 * (1 - i)
            rows = pl.ds(pl.multiple_of(base * TH, QT), QT)
            q = qb[hf, rows, :]
            top = None
            for k in range(NK // KC):
                s = lax.dot_general(
                    q, kb[kh, k * KC : (k + 1) * KC, :], nt, preferred_element_type=F32
                )
                sc[:, k * KC : (k + 1) * KC] = s
                top = s if top is None else jnp.maximum(top, s)
            m = jnp.max(top, axis=1, keepdims=True)
            if kh == 1:
                m0 = am[hf, rows, :]
                m = jnp.maximum(m, m0)
                old = jnp.exp2((m0 - m) * coef)
            tot = None
            out = None
            for k in range(NK // KC):
                p = jnp.exp2((sc[:, k * KC : (k + 1) * KC] - m) * coef)
                o = jnp.dot(
                    p.astype(BF), vb[kh, k * KC : (k + 1) * KC, :], preferred_element_type=F32
                )
                tot = p if tot is None else tot + p
                out = o if out is None else out + o
            tot = jnp.sum(tot, axis=1, keepdims=True)
            if kh == 0:
                am[hf, rows, :] = m
                al[hf, rows, :] = tot
                aa[hf, rows, :] = out
                return 0
            tot = tot + al[hf, rows, :] * old
            out = out + aa[hf, rows, :] * old
            res = (out / tot).astype(BF)
            cs[hf, base] = res[:TH]
            cs[hf, base + 1] = res[TH:]
            for k in (base, base + 1):
                src = rem(y + k, 4)
                remote(
                    cs.at[hf, k], cbx.at[hf, y], XC + hf, k, (part[0], xl * 8 + src * 2 + c)
                ).start()

                @pl.when(k != 0)
                def _():
                    remote(
                        cs.at[hf, k], cb.at[hf, y], CX + hf, k, (me_v, xl * 8 + src * 2 + c)
                    ).start()

            return 0

        lax.fori_loop(0, 2, tile, 0)
        if kh == 1:
            cb[hf, y] = cs[hf, 0]
            for k in range(1, 4):
                src = rem(y + k, 4)
                cp = remote(
                    cs.at[hf, k], cb.at[hf, y], CX + hf, k, (me_v, xl * 8 + src * 2 + c)
                )
                cx_cps[hf].append(cp)
            for k in range(4):
                src = rem(y + k, 4)
                cp = remote(
                    cs.at[hf, k], cbx.at[hf, y], XC + hf, k, (part[0], xl * 8 + src * 2 + c)
                )
                cx_cps[hf].append(cp)
            pending.extend(cx_cps[hf])

    cx_cps = [[], []]

    for hf in range(2):
        shift(hf)
        take(hf, me_v, True)

        def local(i, _, hf=hf):
            take(hf, (1 - xh) * 4 + rem(z + 3 + i, 4))
            return 0

        lax.fori_loop(0, 3, local, 0)

    def arrive(hf):
        for j in reversed(range(4)):
            d_cps[hf][j].wait_recv()
            o = D_OFF[j]
            take(hf, var_of(o, -1))

    arrive(0)
    mean, inv = statistics(0)
    project(0, ks, 0, mean, inv)
    k0 = send_kv(K, ks, kb, 0)
    project(1, vs, 0, mean, inv)
    v0 = send_kv(V, vs, vb, 0)
    project(2, qs, 0, mean, inv)
    q0 = send_q(0)

    arrive(1)
    mean, inv = statistics(1)
    project(0, ks, 1, mean, inv)
    k1 = send_kv(K, ks, kb, 1)
    project(1, vs, 1, mean, inv)
    v1 = send_kv(V, vs, vb, 1)
    project(2, qs, 1, mean, inv)
    q1 = send_q(1)
    k0f = seq_forward(KF, k0, slot(kb, 0))
    v0f = seq_forward(VF, v0, slot(vb, 0))
    pending.extend(k0f + v0f)
    ox.wait_recv()
    ox_sib = remote(
        wox.at[mine_rows, :], wox.at[mine_rows, :], OX, 1, sib
    )
    ox_sib.start()
    pending.append(ox_sib)

    for cp in k0f + v0f + q0:
        cp.wait_recv()
    attend(0, 0)
    k1f = seq_forward(KF + 1, k1, slot(kb, 1))
    v1f = seq_forward(VF + 1, v1, slot(vb, 1))
    pending.extend(k1f + v1f)
    for cp in q1:
        cp.wait_recv()
    attend(1, 0)
    for cp in k1f + v1f:
        cp.wait_recv()
    attend(0, 1)
    attend(1, 1)

    ox_sib.wait_recv()
    f_cps = [[], []]
    for hf in range(2):
        for cp in cx_cps[hf]:
            cp.wait_recv()
        ctx = jnp.concatenate([cb[hf, h] for h in range(4)], axis=1)
        ctx2 = jnp.concatenate([cbx[hf, h] for h in range(4)], axis=1)

        def out_block(zz):
            own = pl.ds(pl.multiple_of(xh * (D // 2) + zz * W, W), W)
            oth = pl.ds(pl.multiple_of(zz * W, W), W)
            return jnp.dot(ctx, wo[:, own], preferred_element_type=F32) + jnp.dot(
                ctx2, wox[:, oth], preferred_element_type=F32
            )

        for j, o in enumerate(Z_OFF):
            fsend[hf, j] = out_block(rem(z + o[1], 4)).astype(BF)
            cp = remote(fsend.at[hf, j], frecv.at[hf, j], F + hf, j, (var_of(o), me_s))
            cp.start()
            f_cps[hf].append(cp)
        pending.extend(f_cps[hf])
        fown[hf] = out_block(z) + hid[hf, me_v].astype(F32)

    loads["wb"].wait()
    g_cps = []
    gg_cps = []

    def mix_and_back(hf):
        for cp in f_cps[hf]:
            cp.wait_recv()

        def mix(r, _):
            rows = pl.ds(pl.multiple_of(r * 32, 32), 32)
            s = fown[hf, rows, :]
            for j in range(3):
                s = s + frecv[hf, j, rows, :].astype(F32)
            mixed_r[pl.ds(pl.multiple_of(hf * TH + r * 32, 32), 32), :] = s.astype(BF)
            return 0

        lax.fori_loop(0, TH // 32, mix, 0)
        mx = mixed_r[hf * TH : (hf + 1) * TH, :]
        for p in range(0, NV, 2):
            g = jnp.dot(mx, wb[:, p * 128 : (p + 2) * 128], preferred_element_type=F32)
            gsend[hf, p] = g[:, :128].astype(BF)
            gsend[hf, p + 1] = g[:, 128:].astype(BF)
        g_cps.append(var_scatter(G + hf, gsend.at[hf], grecv.at[hf]))

    def back_sum(hf):
        tot = gsend[hf, me_v].astype(F32)
        for j in reversed(range(7)):
            g_cps[hf][j].wait_recv()
            tot = tot + grecv[hf, j].astype(F32)
        gb[hf, me_v] = tot.astype(BF)
        gg_cps.append(var_gather(GG + hf, gb.at[hf]))

    def back_rows(hf):
        for cp in gg_cps[hf]:
            cp.wait_recv()
        for p in range(NV):
            back_r[hf * TH : (hf + 1) * TH, p * 128 : (p + 1) * 128] = gb[hf, p].astype(F32)

    mix_and_back(0)
    mix_and_back(1)
    back_sum(0)
    back_sum(1)
    back_rows(0)
    back_rows(1)

    for cp in pending:
        cp.wait_send()


def per_device(
    fields, var_bias, agg_score, agg_value, agg_out, norm_gain,
    w_query, w_key, w_value, w_out, w_back, var_gate,
):
    any_spec = pl.BlockSpec(memory_space=pl.ANY)
    vm = pl.BlockSpec(memory_space=pltpu.VMEM)
    mixed, back, gate = pl.pallas_call(
        body,
        out_shape=(
            jax.ShapeDtypeStruct((T, W), BF),
            jax.ShapeDtypeStruct((T, E), F32),
            jax.ShapeDtypeStruct((LV, E), F32),
        ),
        in_specs=[
            any_spec, vm, vm, any_spec, any_spec, vm,
            any_spec, any_spec, any_spec, any_spec, any_spec, vm,
        ],
        out_specs=(vm, vm, vm),
        scratch_shapes=[
            pltpu.VMEM((LV, T, E), BF),
            pltpu.VMEM((E, E), BF),
            pltpu.VMEM((E, W), BF),
            pltpu.VMEM((4, E, W), BF),
            pltpu.VMEM((D, W), BF),
            pltpu.VMEM((D, W), BF),
            pltpu.VMEM((D, W), BF),
            pltpu.VMEM((W, D), BF),
            pltpu.VMEM((W, D // 2), BF),
            pltpu.VMEM((W, E), BF),
            pltpu.VMEM((128, E), BF),
            pltpu.VMEM((LV, T, HA), F32),
            pltpu.VMEM((NV, 32, T), F32),
            pltpu.VMEM((LV, T, 128), BF),
            pltpu.VMEM((2, NV, TH, 128), BF),
            pltpu.VMEM((2, 7, TH, 128), BF),
            pltpu.VMEM((2, NV, TH, 128), BF),
            pltpu.VMEM((2, NV, TH, W), BF),
            pltpu.VMEM((2, 3, TH, W), F32),
            pltpu.VMEM((NV, 8, W), F32),
            pltpu.VMEM((3, 1, W), F32),
            pltpu.VMEM((2, TH, 1), F32),
            pltpu.VMEM((2, TH, 128), F32),
            pltpu.VMEM((2, TH, 128), F32),
            pltpu.VMEM((2, 4, TH, HD), BF),
            pltpu.VMEM((2, 4, TH, HD), BF),
            pltpu.VMEM((2, 4, TH, HD), BF),
            pltpu.VMEM((2, NS * TH, HD), BF),
            pltpu.VMEM((2, NS * TH, HD), BF),
            pltpu.VMEM((2, 4 * TH, HD), BF),
            pltpu.VMEM((2 * TH, NS * TH), F32),
            pltpu.VMEM((2, 4 * TH, 1), F32),
            pltpu.VMEM((2, 4 * TH, 1), F32),
            pltpu.VMEM((2, 4 * TH, HD), F32),
            pltpu.VMEM((2, 4, TH, HD), BF),
            pltpu.VMEM((2, 4, TH, HD), BF),
            pltpu.VMEM((2, 4, TH, HD), BF),
            pltpu.VMEM((2, 3, TH, W), BF),
            pltpu.VMEM((2, 3, TH, W), BF),
            pltpu.VMEM((2, TH, W), F32),
            pltpu.VMEM((2, NV, TH, 128), BF),
            pltpu.VMEM((2, 7, TH, 128), BF),
            pltpu.VMEM((2, NV, TH, 128), BF),
            pltpu.SemaphoreType.DMA((8,)),
            pltpu.SemaphoreType.DMA((ROWS, 8)),
            pltpu.SemaphoreType.DMA((ROWS, 8)),
        ],
        compiler_params=pltpu.CompilerParams(
            collective_id=0, has_side_effects=True, vmem_limit_bytes=60 * 2**20
        ),
    )(
        fields, var_bias, agg_score.T, agg_value, agg_out, norm_gain,
        w_query, w_key, w_value, w_out, w_back, var_gate,
    )
    out_fields = (fields.astype(F32) + gate[:, None, :] * back[None]).astype(BF)
    return (mixed, out_fields)


def solution(mesh):
    in_specs = (
        P("var", "seq", None),
        P("var", None),
        P(),
        P("seq", None),
        P(None, "var"),
        P(),
        P(None, "var"),
        P(None, "var"),
        P(None, "var"),
        P("var", None),
        P("var", None),
        P("var", None),
    )
    out_specs = (P("seq", "var"), P("var", "seq", None))
    return jax.shard_map(
        per_device, mesh=mesh, in_specs=in_specs, out_specs=out_specs, check_vma=False
    )
```

time: 567 us -> 122 us (0.22)
  waiting for transfers between devices: 344 us -> 0 us
  Pallas kernels: 0 us -> 117 us
  blocking collectives: 69.7 us -> 0 us
  matrix products: 48.3 us -> 0 us
  local copies, waits for them, and re-layouts: 43.4 us -> 0.71 us
  other arithmetic: 45.6 us -> 3.9 us
  between operations: 14.3 us -> 0.67 us
    all_gather x5 -> x0, waiting for transfers between devices: 171 us -> none  [the longest x1 52.4 us: per_device(): hidden = lax.all_gather(own_hidden, 'var', axis=1, tiled=True)]
    pallas_call x0 -> x1, Pallas kernels: none -> 117 us  [per_device(): pl.pallas_call(body, out_shape=(jax.ShapeDtypeStruct((T, W), BF), jax.Sha...]
    psum x1 -> x0, waiting for transfers between devices: 87.3 us -> none  [per_device(): back = lax.psum(back_part, 'var')]
    reduce_scatter x1 -> x0, waiting for transfers between devices: 84.8 us -> none  [per_device(): lax.psum_scatter(partial_out, 'var', scatter_dimension=1, tiled=True)]
    all_gather x2 -> x0, blocking collectives: 69.7 us -> none  [joined(): pieces = jax.tree.map(lambda part: lax.all_gather(part, axis), value)]
    dot_general x10 -> x0, matrix products: 48.3 us -> none  [the longest x1 10.6 us: per_device(): jnp.einsum('hts,shd->thd', expo.astype(jnp.bfloat16), all_vals, preferred...]
    add x14 -> x0, other arithmetic: 16.6 us -> none  [the longest x7 16.4 us: combine_partials(): first[2] * jnp.repeat(scale_one, reach, axis=1)]
    reshape x2 -> x0, local copies, waits for them, and re-layouts: 13.9 us -> none  [the longest x1 7.49 us: per_device(): values = values.reshape(var_count, tok_count, HA, agg_dim)]
  transfers between devices with their start and end apart: 7 -> 0, of which waited for: 7 -> 0; matrix products, arithmetic and copies ran while one was open for 6% -> 0% of each run, Pallas kernels for 0% -> 0%
where the time goes in v1:
time: 122 us
  Pallas kernels  117 us (96%)
  other arithmetic  3.9 us (3%)
    pallas_call x1, Pallas kernels, per_device(): pl.pallas_call(body, out_shape=(jax.ShapeDtypeStruct((T, W), BF), jax.Sha...  117 us
    convert_element_type x1, other arithmetic, per_device(): out_fields = (fields.astype(F32) + gate[:, None, :] * back[None]).astype(BF)  3.9 us

profile of v1, /device:TPU:0, one launch (start us, length us, event | category | flops | bytes accessed | tf_op | source)
XLA Modules:
  0.0 122.1 jit_solution(10640841152240503418)
XLA Ops:
  0.6 0.0 copy-start
  0.6 116.8 %shard_map.131 = (bf16[256,512]{1,0:T(8,128)(2,1)}, f32[256,1024]{1,0:T(8,128)}, f32[6,1024]{1,0:T(8,128)}) custom-call(bf16[6,256,1024]{2,1,0:T(8,128)(2,1)} %fields_h.1, bf16[6,1024]{1,0:T(8,128)(2,1)} %bias_r.1, bf16[16,1024]{1,0:T(8,128)(2,1)} %bitcast.1, bf16[64,1024]{1,0:T(8,128)(2,1)} %av_h.1, bf16[1024,512]{1,0:T(8,128)(2,1)} %ao_h.1, f32[4096]{0:T(1024)} %gain_r.1, ...), custom_call_target="tpu_custom_call" | custom-call | tf_op jit(solution)/shard_map/pallas_call | solution.py:591
  117.5 0.0 copy-start.1
  117.5 0.0 copy-done
  117.5 3.9 %add_convert_fusion = bf16[6,256,1024]{2,1,0:T(8,128)(2,1)} fusion(bf16[6,256,1024]{2,1,0:T(8,128)(2,1)S(1)} %copy-done, f32[256,1024]{1,0:T(8,128)} %get-tuple-element.7, f32[6,1024]{1,0:T(8,128)} %get-tuple-element.6), kind=kLoop, calls=%fused_computation | loop fusion | flops 6291456 | bytes 7364608 | tf_op jit(solution)/shard_map/convert_element_type | solution.py:658
  121.4 0.0 copy-done.1
  121.4 0.7 copy.15
Async XLA Ops:
  0.6 116.8 %copy-start = (bf16[6,256,1024]{2,1,0:T(8,128)(2,1)S(1)}, bf16[6,256,1024]{2,1,0:T(8,128)(2,1)}, u32[]{:S(2)}) copy-start(bf16[6,256,1024]{2,1,0:T(8,128)(2,1)} %fields_h.1) | copy-start | bytes 9437188
  117.5 3.9 %copy-start.1 = (bf16[256,512]{1,0:T(8,128)(2,1)S(1)}, bf16[256,512]{1,0:T(8,128)(2,1)}, u32[]{:S(2)}) copy-start(bf16[256,512]{1,0:T(8,128)(2,1)} %get-tuple-element.10) | copy-start | bytes 786436
